TPU v7x, 128 devices: a whole 4x4x4 slice. The times are simulated.
128 devices in a mesh: rep: 4 (over x), space: 32 (over z, y, core).
Axes of the slice: x: 4, y: 4, z: 4, core: 2. Of those that a mesh axis runs over, the one named last changes fastest.
Arguments:
- latents: bfloat16 [512, 512, 256], P(('rep', 'space')), may hold values from -6 to 6
- cotangent: bfloat16 [512, 512, 256], P(('rep', 'space')), may hold values from -6 to 6
- w_up: bfloat16 [2, 256, 1024], replicated, may hold values from -0.375 to 0.375
- w_down: bfloat16 [2, 1024, 256], replicated, may hold values from -0.1875 to 0.1875
- depth_w: float32 [2, 7, 256], replicated, may hold values from -2 to 2
- time_table: float32 [1000, 256], replicated, may hold values from -6 to 6
- timesteps: int32 [4], P('rep'), may hold values from 0 to 999
- brick_counts: int32 [128], P(('rep', 'space')), may hold values from 1 to 4, as said below
- send_list: int32 [128, 2, 2], P(('rep', 'space')), may hold values from 0 to 13, as said below
- recv_list: int32 [512, 4], P(('rep', 'space')), may hold values from 0 to 20, as said below
Outputs:
- d_latents: bfloat16 [512, 512, 256], P(('rep', 'space'))
- grad_up: float32 [2, 256, 1024], P(None, None, 'rep')
- grad_down: float32 [2, 1024, 256], P(None, 'rep')
- grad_depth: float32 [2, 7, 256], P(None, None, 'rep')
Inputs may be any that keep to these rules, and one draw needn't show every extreme that they name: `brick_counts`: some device of every scene holds 4 bricks and some holds one. `send_list`: entry 4 s + f names face f of local slot s; list 0 goes to the device below along space, list 1 to the device above. `recv_list`: 0 means no neighbour, 1 + 4 s + f face f of local slot s, 17 + e entry e received from the device below, 19 + e entry e from the device above. Empty slots have 0 on every side. Whenever a slot names a face across a side, the brick of that face names this slot's facing face across the opposite side.
All inputs are finite; a program needn't handle non-finite values.
Results may differ from a plain program's by a relative error of at most 0.035.
Values may be sent and summed in bfloat16 or wider, within the bound.
A program may use at most 128 MiB of HBM per device.

v0:
```python
import math
import jax
import jax.numpy as jnp
from jax import lax
from jax.sharding import PartitionSpec as P

E = 8
CUBIC = 0.044715
ROOT = math.sqrt(2.0 / math.pi)
FORWARD_ORDER = (0, 1, 2, 3, 4, 5, 6)
MIRROR_ORDER = (0, 2, 1, 4, 3, 6, 5)


def from_behind(value, axis, steps):
    count = lax.axis_size(axis)
    initial, last = (max(0, -steps), min(count, count - steps))
    return lax.ppermute(value, axis, [(source, source + steps) for source in range(initial, last)])


def gelu_tanh(values):
    return 0.5 * values * (1.0 + jnp.tanh(ROOT * (values + CUBIC * values * values * values)))


def gelu_slope(values):
    inner = jnp.tanh(ROOT * (values + CUBIC * values * values * values))
    return 0.5 * (1.0 + inner) + 0.5 * values * (1.0 - inner * inner) * ROOT * (
        1.0 + 3.0 * CUBIC * values * values
    )


def planes_of(fields):
    count = fields.shape[0]
    cube = fields.reshape(count, E, E, E, fields.shape[-1])
    stacked = jnp.stack([cube[:, 0], cube[:, E - 1], cube[:, :, 0], cube[:, :, E - 1]], axis=1)
    return stacked.reshape(count * 4, E * E, fields.shape[-1])


def neighbours(field, ghosts):
    count = field.shape[0]
    width = field.shape[-1]
    cube = field.reshape(count, E, E, E, width).astype(jnp.float32)
    sides = ghosts.reshape(count, 4, E, E, width).astype(jnp.float32)
    along_x = jnp.concatenate([sides[:, 0:1], cube, sides[:, 1:2]], axis=1)
    along_y = jnp.concatenate([sides[:, 2][:, :, None], cube, sides[:, 3][:, :, None]], axis=2)
    along_z = jnp.pad(cube, ((0, 0), (0, 0), (0, 0), (1, 1), (0, 0)))
    pieces = [
        cube,
        along_x[:, :-2],
        along_x[:, 2:],
        along_y[:, :, :-2],
        along_y[:, :, 2:],
        along_z[:, :, :, :-2],
        along_z[:, :, :, 2:],
    ]
    return [piece.reshape(-1, width) for piece in pieces]


def combine(fields, weights, order):
    total = weights[order[0]][None, :] * fields[0]
    for index in range(1, 7):
        total = total + weights[order[index]][None, :] * fields[index]
    return total


def trade_faces(fields, sends, recvs):
    copies, bricks, voxels, channels = fields.shape
    planes = planes_of(fields.reshape(copies * bricks, voxels, channels)).reshape(
        copies, bricks * 4, E * E, channels
    )
    outgoing = planes[:, sends.reshape(-1)].reshape(copies, 2, sends.shape[1], E * E, channels)
    from_lower = from_behind(outgoing[:, 1], "space", 1)
    from_upper = from_behind(outgoing[:, 0], "space", -1)
    blank = jnp.zeros((copies, 1, E * E, channels), jnp.bfloat16)
    face_pool = jnp.concatenate([blank, planes, from_lower, from_upper], axis=1)
    return face_pool[:, recvs.reshape(-1)].reshape(copies, bricks, 4, E * E, channels)


def on_device(
    latents,
    cotangent,
    w_up,
    w_down,
    depth_w,
    time_table,
    timesteps,
    brick_counts,
    send_list,
    recv_list,
):
    bricks, voxels, channels = latents.shape
    blocks = w_up.shape[0]
    sends = send_list[0]
    occupied = (jnp.arange(bricks, dtype=jnp.int32) < brick_counts[0]).astype(jnp.float32)[
        :, None, None
    ]
    time_shift = time_table[timesteps[0]]
    field = (latents.astype(jnp.float32) * occupied).astype(jnp.bfloat16)
    saved = []
    for block in range(blocks):
        ghosts = trade_faces(field[None], sends, recv_list)[0]
        near = neighbours(field, ghosts)
        activation = (combine(near, depth_w[block], FORWARD_ORDER) + time_shift[None, :]).astype(
            jnp.bfloat16
        )
        preact = jnp.dot(activation, w_up[block], preferred_element_type=jnp.float32)
        hidden = gelu_tanh(preact).astype(jnp.bfloat16)
        summed = field.reshape(-1, channels).astype(jnp.float32) + jnp.dot(
            hidden, w_down[block], preferred_element_type=jnp.float32
        )
        saved.append((field, ghosts, activation, preact, hidden))
        field = (summed.reshape(bricks, voxels, channels) * occupied).astype(jnp.bfloat16)
    grad = (cotangent.astype(jnp.float32) * occupied).astype(jnp.bfloat16)
    parts_up = [None] * blocks
    parts_down = [None] * blocks
    parts_depth = [None] * blocks
    contract_rows = (((0,), (0,)), ((), ()))
    contract_cols = (((1,), (1,)), ((), ()))
    for block in range(blocks - 1, -1, -1):
        field_in, ghosts_in, activation, preact, hidden = saved[block]
        flat_grad = grad.reshape(-1, channels)
        parts_down[block] = lax.dot_general(
            hidden, flat_grad, contract_rows, preferred_element_type=jnp.float32
        )
        d_hidden = lax.dot_general(
            flat_grad, w_down[block], contract_cols, preferred_element_type=jnp.float32
        )
        d_preact = (d_hidden * gelu_slope(preact)).astype(jnp.bfloat16)
        parts_up[block] = lax.dot_general(
            activation, d_preact, contract_rows, preferred_element_type=jnp.float32
        )
        d_act = lax.dot_general(
            d_preact, w_up[block], contract_cols, preferred_element_type=jnp.float32
        ).astype(jnp.bfloat16)
        d_field = d_act.reshape(bricks, voxels, channels)
        ghosts_grad = trade_faces(d_field[None], sends, recv_list)[0]
        near_in = neighbours(field_in, ghosts_in)
        d_wide = d_act.astype(jnp.float32)
        parts_depth[block] = jnp.stack([jnp.sum(piece * d_wide, axis=0) for piece in near_in])
        back = combine(neighbours(d_field, ghosts_grad), depth_w[block], MIRROR_ORDER)
        total = flat_grad.astype(jnp.float32) + back
        grad = (total.reshape(bricks, voxels, channels) * occupied).astype(jnp.bfloat16)
    local_up = jnp.stack(parts_up)
    local_down = jnp.stack(parts_down)
    local_depth = jnp.stack(parts_depth)
    whole = (
        lax.psum(local_up.astype(jnp.bfloat16), "space").astype(jnp.float32),
        lax.psum(local_down.astype(jnp.bfloat16), "space").astype(jnp.float32),
        lax.psum(local_depth.astype(jnp.bfloat16), "space").astype(jnp.float32),
    )
    sum_up, sum_down, sum_depth = (
        lax.psum_scatter(
            whole[0].astype(jnp.bfloat16), "rep", scatter_dimension=2, tiled=True
        ).astype(jnp.float32),
        lax.psum_scatter(
            whole[1].astype(jnp.bfloat16), "rep", scatter_dimension=1, tiled=True
        ).astype(jnp.float32),
        lax.psum_scatter(
            whole[2].astype(jnp.bfloat16), "rep", scatter_dimension=2, tiled=True
        ).astype(jnp.float32),
    )
    scale = 1.0 / math.sqrt(bricks * lax.axis_size("rep") * lax.axis_size("space") * voxels)
    return (grad, sum_up * scale, sum_down * scale, sum_depth * scale)


def solution(mesh):
    return jax.shard_map(
        on_device,
        mesh=mesh,
        in_specs=(
            P(("rep", "space"), None, None),
            P(("rep", "space"), None, None),
            P(),
            P(),
            P(),
            P(),
            P("rep"),
            P(("rep", "space")),
            P(("rep", "space"), None, None),
            P(("rep", "space"), None),
        ),
        out_specs=(
            P(("rep", "space"), None, None),
            P(None, None, "rep"),
            P(None, "rep", None),
            P(None, None, "rep"),
        ),
        check_vma=False,
    )
```

profile of v0, /device:TPU:1, one launch (start us, length us, event | category | flops | bytes accessed | tf_op | source)
XLA Modules:
  0.0 312.6 jit_solution(17737770641990076478)
XLA Ops:
  8.0 3.4 %multiply_convert_fusion.6 = (bf16[4,512,256]{2,1,0:T(8,128)(2,1)}, bf16[4,512,256]{2,1,0:T(8,128)(2,1)S(1)}) fusion(bf16[4,512,256]{2,1,0:T(8,128)(2,1)} %param.11, f32[4]{0:T(128)S(1)} %compare_convert_fusion, bf16[4,512,256]{2,1,0:T(8,128)(2,1)} %param.10), kind=kLoop, calls=%fused_computation.163 | loop fusion | flops 3145728 | bytes 4194320 | tf_op jit(solution)/shard_map/convert_element_type | solution.py:112
  12.3 4.6 %collective-permute-start = (bf16[1,2,64,256]{3,2,1,0:T(8,128)(2,1)S(1)}, bf16[1,2,64,256]{3,2,1,0:T(8,128)(2,1)S(1)}, u32[]{:S(2)}, u32[]{:S(2)}) collective-permute-start(bf16[1,2,64,256]{3,2,1,0:T(8,128)(2,1)S(1)} %get-tuple-element.97), channel_id=1, source_target_pairs={{0,1},{1,2},{2,3},{3,4},{4,5},{5,6},{6,7},{7,8},{8,9},{9,10},{10,1... | collective-permute-start | bytes 196616 | tf_op jit(solution)/shard_map/ppermute | solution.py:17
  32.3 3.0 convolution_add_fusion
  37.8 2.5 collective-permute-start.2
  40.3 2.1 collective-permute-start.3
  42.6 3.2 %collective-permute-done.3 = bf16[1,2,64,256]{3,2,1,0:T(8,128)(2,1)S(1)} collective-permute-done((bf16[1,2,64,256]{3,2,1,0:T(8,128)(2,1)S(1)}, bf16[1,2,64,256]{3,2,1,0:T(8,128)(2,1)S(1)}, u32[]{:S(2)}, u32[]{:S(2)}) %collective-permute-start.3) | collective-permute-done | bytes 65568 | tf_op jit(solution)/shard_map/ppermute | solution.py:17
  53.6 2.2 fusion.22
  57.8 5.9 %fusion.8 = bf16[2048,1024]{1,0:T(8,128)(2,1)S(1)} fusion(f32[2048,1024]{1,0:T(8,128)S(1)} %fusion.76, bf16[2048,256]{1,0:T(8,128)(2,1)S(1)} %bitcast.382, bf16[2,1024,256]{2,1,0:T(8,128)(2,1)S(1)} %copy-done.41), kind=kOutput, calls=%fused_computation.20 | convolution fusion | flops 1113587712 | bytes 14155776 | tf_op jit(solution)/shard_map/dot_general | solution.py:124
  63.7 4.2 %fusion.38 = (bf16[256]{0:T(256)(128)(2,1)S(1)}, bf16[256]{0:T(256)(128)(2,1)S(1)}, bf16[256]{0:T(256)(128)(2,1)S(1)}, bf16[256]{0:T(256)(128)(2,1)S(1)}, bf16[2...) fusion(f32[4,8,8,8,256]{4,3,2,1,0:T(8,128)S(1)} %copy.124, ...), kind=kOutput, calls=%fused_computation.80 | convolution fusion | flops 1083701504 | bytes 20459008 | tf_op jit(solution)/shard_map/dot_general | solution.py:131
  69.7 1.9 collective-permute-start.4
  71.6 2.8 collective-permute-start.5
  74.4 6.1 %fusion.71 = bf16[1,1024,256]{2,1,0:T(8,128)(2,1)} fusion(bf16[2048,256]{1,0:T(8,128)(2,1)S(1)} %bitcast.383, f32[2048,1024]{1,0:T(8,128)} %copy-done.3), kind=kOutput, calls=%fused_computation.168 | convolution fusion | flops 1092878336 | bytes 9961472 | tf_op jit(solution)/shard_map/dot_general | solution.py:121
  88.2 2.2 fusion.31
  90.5 3.6 %fusion.74 = bf16[1,1024,256]{2,1,0:T(8,128)(2,1)S(1)} fusion(bf16[2048,256]{1,0:T(8,128)(2,1)S(1)} %fusion.31, f32[2048,1024]{1,0:T(8,128)S(1)} %bitcast.361), kind=kOutput, calls=%fused_computation.171 | convolution fusion | flops 1092878336 | bytes 9961472 | tf_op jit(solution)/shard_map/dot_general | solution.py:121
  94.2 5.9 %fusion.13 = bf16[2048,1024]{1,0:T(8,128)(2,1)S(1)} fusion(f32[2048,1024]{1,0:T(8,128)S(1)} %bitcast.361, bf16[2048,256]{1,0:T(8,128)(2,1)S(1)} %fusion.31, bf16[2,1024,256]{2,1,0:T(8,128)(2,1)S(1)} %copy-done.42), kind=kOutput, calls=%fused_computation.25 | convolution fusion | flops 1113587712 | bytes 14155776 | tf_op jit(solution)/shard_map/dot_general | solution.py:124
  100.2 5.9 %fusion.52 = (bf16[256]{0:T(256)(128)(2,1)S(1)}, bf16[256]{0:T(256)(128)(2,1)S(1)}, bf16[256]{0:T(256)(128)(2,1)S(1)}, bf16[256]{0:T(256)(128)(2,1)S(1)}, bf16[2...) fusion(f32[4,8,8,8,256]{4,3,2,1,0:T(8,128)S(1)} %copy-done.12, ...), kind=kOutput, calls=%fused_computation.94 | convolution fusion | flops 1090517248 | bytes 20459008 | tf_op jit(solution)/shard_map/dot_general | solution.py:131
  108.4 4.3 %fusion.73 = bf16[1,256,1024]{2,1,0:T(8,128)(2,1)} fusion(bf16[2048,256]{1,0:T(8,128)(2,1)S(1)} %copy-done.27, bf16[2048,1024]{1,0:T(8,128)(2,1)} %copy-done.32), kind=kOutput, calls=%fused_computation.170 | convolution fusion | flops 1074003968 | bytes 5767168 | tf_op jit(solution)/shard_map/dot_general | solution.py:128
  113.7 3.1 %collective-permute-start.6 = (bf16[1,2,64,256]{3,2,1,0:T(8,128)(2,1)S(1)}, bf16[1,2,64,256]{3,2,1,0:T(8,128)(2,1)S(1)}, u32[]{:S(2)}, u32[]{:S(2)}) collective-permute-start(bf16[1,2,64,256]{3,2,1,0:T(8,128)(2,1)S(1)} %get-tuple-element.91), channel_id=1, source_target_pairs={{0,1},{1,2},{2,3},{3,4},{4,5},{5,6},{6,7},{7,8},{8,9},{9,10},{10,1... | collective-permute-start | bytes 196616 | tf_op jit(solution)/shard_map/ppermute | solution.py:17
  116.9 2.2 collective-permute-start.7
  119.1 3.8 %fusion.72 = bf16[1,256,1024]{2,1,0:T(8,128)(2,1)S(1)} fusion(bf16[2048,256]{1,0:T(8,128)(2,1)} %get-tuple-element.34, bf16[2048,1024]{1,0:T(8,128)(2,1)} %copy-done.44), kind=kOutput, calls=%fused_computation.169 | convolution fusion | flops 1074003968 | bytes 5767168 | tf_op jit(solution)/shard_map/dot_general | solution.py:128
  124.1 6.8 %reduce-scatter.10.cloned.1.call-done = bf16[64,14]{1,0:T(8,128)(2,1)} async-done(((bf16[256,14]{1,0:T(8,128)(2,1)}), bf16[64,14]{1,0:T(8,128)(2,1)}) %reduce-scatter.10.cloned.1.call-update) | async-done | bytes 1808
  131.7 65.2 %psum.26 = bf16[2,7,64]{2,1,0:T(8,128)(2,1)S(1)} all-reduce(bf16[2,7,64]{2,1,0:T(8,128)(2,1)S(1)} %copy.135), channel_id=1, replica_groups=mesh['rep'=4,'space'=32] {'space'}, use_global_device_ids=true, to_apply=%region_18.19 | all-reduce | flops 896 | bytes 3584 | tf_op jit(solution)/shard_map/psum | solution.py:148
  204.4 99.6 %all-reduce.7.cloned.1.call-done = (bf16[2,256,256]{2,1,0:T(8,128)(2,1)}, bf16[2,256,256]{2,1,0:T(8,128)(2,1)}) async-done(((bf16[2,256,256]{2,1,0:T(8,128)(2,1)}, bf16[2,256,256]{2,1,0:T(8,128)(2,1)}), (bf16[2,256,256]{2,1,0:T(8,128)(2,1)}, bf16[2,256,256]{2,1,0:T(8,128)(2,1)})) %all-reduce.7.cloned.1.call-update) | async-done | bytes 524304 | tf_op jit(solution)/shard_map/psum | solution.py:146
  304.0 2.1 convert_multiply_fusion.17
  (212 shorter events, 49.6 us)
Async XLA Ops:
  7.2 14.1 %copy-start = (f32[1000,256]{1,0:T(8,128)S(1)}, f32[1000,256]{1,0:T(8,128)}, u32[]{:S(2)}) copy-start(f32[1000,256]{1,0:T(8,128)} %param.15) | copy-start | bytes 3072004
  7.2 123.6 %reduce-scatter.10.cloned.1.call-start = ((), (), s32[]{:S(2)}) async-start(), calls=%async_computation.5 | async-start | bytes 81920
  11.4 14.9 %copy-start.4 = (bf16[4,512,256]{2,1,0:T(8,128)(2,1)}, bf16[4,512,256]{2,1,0:T(8,128)(2,1)S(1)}, u32[]{:S(2)}) copy-start(bf16[4,512,256]{2,1,0:T(8,128)(2,1)S(1)} %get-tuple-element.114) | copy-start | bytes 3145732
  11.7 9.4 %copy-start.39 = (s32[4,4]{1,0:T(4,128)S(1)}, s32[4,4]{1,0:T(4,128)}, u32[]{:S(2)}) copy-start(s32[4,4]{1,0:T(4,128)} %param.19) | copy-start | bytes 196
  11.7 9.5 %copy-start.38 = (f32[2,7,256]{2,0,1:T(2,128)S(1)}, f32[2,7,256]{2,0,1:T(2,128)}, u32[]{:S(2)}) copy-start(f32[2,7,256]{2,0,1:T(2,128)} %param.14) | copy-start | bytes 43012
  12.3 9.0 %collective-permute-start = (bf16[1,2,64,256]{3,2,1,0:T(8,128)(2,1)S(1)}, bf16[1,2,64,256]{3,2,1,0:T(8,128)(2,1)S(1)}, u32[]{:S(2)}, u32[]{:S(2)}) collective-permute-start(bf16[1,2,64,256]{3,2,1,0:T(8,128)(2,1)S(1)} %get-tuple-element.97), channel_id=1, source_target_pairs={{0,1},{1,2},{2,3},{3,4},{4,5},{5,6},{6,7},{7,8},{8,9},{9,10},{10,1... | collective-permute-start | bytes 196616 | tf_op jit(solution)/shard_map/ppermute | solution.py:17
  16.9 5.6 %collective-permute-start.1 = (bf16[1,2,64,256]{3,2,1,0:T(8,128)(2,1)S(1)}, bf16[1,2,64,256]{3,2,1,0:T(8,128)(2,1)S(1)}, u32[]{:S(2)}, u32[]{:S(2)}) collective-permute-start(bf16[1,2,64,256]{3,2,1,0:T(8,128)(2,1)S(1)} %get-tuple-element.98), channel_id=1, source_target_pairs={{1,0},{2,1},{3,2},{4,3},{5,4},{6,5},{7,6},{8,7},{9,8},{10,9},{11,1... | collective-permute-start | bytes 196616 | tf_op jit(solution)/shard_map/ppermute | solution.py:17
  37.8 4.8 %collective-permute-start.2 = (bf16[1,2,64,256]{3,2,1,0:T(8,128)(2,1)S(1)}, bf16[1,2,64,256]{3,2,1,0:T(8,128)(2,1)S(1)}, u32[]{:S(2)}, u32[]{:S(2)}) collective-permute-start(bf16[1,2,64,256]{3,2,1,0:T(8,128)(2,1)S(1)} %get-tuple-element.95), channel_id=1, source_target_pairs={{0,1},{1,2},{2,3},{3,4},{4,5},{5,6},{6,7},{7,8},{8,9},{9,10},{10,1... | collective-permute-start | bytes 196616 | tf_op jit(solution)/shard_map/ppermute | solution.py:17
  40.3 5.6 %collective-permute-start.3 = (bf16[1,2,64,256]{3,2,1,0:T(8,128)(2,1)S(1)}, bf16[1,2,64,256]{3,2,1,0:T(8,128)(2,1)S(1)}, u32[]{:S(2)}, u32[]{:S(2)}) collective-permute-start(bf16[1,2,64,256]{3,2,1,0:T(8,128)(2,1)S(1)} %get-tuple-element.96), channel_id=1, source_target_pairs={{1,0},{2,1},{3,2},{4,3},{5,4},{6,5},{7,6},{8,7},{9,8},{10,9},{11,1... | collective-permute-start | bytes 196616 | tf_op jit(solution)/shard_map/ppermute | solution.py:17
  57.2 6.5 %copy-start.3 = (f32[2048,1024]{1,0:T(8,128)}, f32[2048,1024]{1,0:T(8,128)S(1)}, u32[]{:S(2)}) copy-start(f32[2048,1024]{1,0:T(8,128)S(1)} %fusion.76) | copy-start | bytes 25165828
  68.0 6.4 %copy-start.29 = (bf16[4,512,256]{2,1,0:T(8,128)(2,1)S(1)}, bf16[4,512,256]{2,1,0:T(8,128)(2,1)}, u32[]{:S(2)}) copy-start(bf16[4,512,256]{2,1,0:T(8,128)(2,1)} %get-tuple-element.113) | copy-start | bytes 3145732
  69.7 12.5 %collective-permute-start.4 = (bf16[1,2,64,256]{3,2,1,0:T(8,128)(2,1)S(1)}, bf16[1,2,64,256]{3,2,1,0:T(8,128)(2,1)S(1)}, u32[]{:S(2)}, u32[]{:S(2)}) collective-permute-start(bf16[1,2,64,256]{3,2,1,0:T(8,128)(2,1)S(1)} %get-tuple-element.93), channel_id=1, source_target_pairs={{0,1},{1,2},{2,3},{3,4},{4,5},{5,6},{6,7},{7,8},{8,9},{9,10},{10,1... | collective-permute-start | bytes 196616 | tf_op jit(solution)/shard_map/ppermute | solution.py:17
  71.6 8.9 %copy-start.8 = (bf16[2048,256]{1,0:T(8,128)(2,1)S(1)}, bf16[2048,256]{1,0:T(8,128)(2,1)}, u32[]{:S(2)}) copy-start(bf16[2048,256]{1,0:T(8,128)(2,1)} %copy-done.7) | copy-start | bytes 3145732
  71.6 10.5 %collective-permute-start.5 = (bf16[1,2,64,256]{3,2,1,0:T(8,128)(2,1)S(1)}, bf16[1,2,64,256]{3,2,1,0:T(8,128)(2,1)S(1)}, u32[]{:S(2)}, u32[]{:S(2)}) collective-permute-start(bf16[1,2,64,256]{3,2,1,0:T(8,128)(2,1)S(1)} %get-tuple-element.94), channel_id=1, source_target_pairs={{1,0},{2,1},{3,2},{4,3},{5,4},{6,5},{7,6},{8,7},{9,8},{10,9},{11,1... | collective-permute-start | bytes 196616 | tf_op jit(solution)/shard_map/ppermute | solution.py:17
  94.1 6.0 %copy-start.6 = (bf16[4,512,256]{2,1,0:T(8,128)(2,1)S(1)}, bf16[4,512,256]{2,1,0:T(8,128)(2,1)}, u32[]{:S(2)}) copy-start(bf16[4,512,256]{2,1,0:T(8,128)(2,1)} %copy-done.4) | copy-start | bytes 3145732
  94.1 6.0 %copy-start.10 = (f32[4,8,8,8,256]{4,3,2,1,0:T(8,128)S(1)}, f32[4,8,8,8,256]{4,3,2,1,0:T(8,128)}, u32[]{:S(2)}) copy-start(f32[4,8,8,8,256]{4,3,2,1,0:T(8,128)} %copy-done.9) | copy-start | bytes 6291460
  94.1 6.0 %copy-start.12 = (f32[4,8,8,8,256]{4,3,2,1,0:T(8,128)S(1)}, f32[4,8,8,8,256]{4,3,2,1,0:T(8,128)}, u32[]{:S(2)}) copy-start(f32[4,8,8,8,256]{4,3,2,1,0:T(8,128)} %copy-done.11) | copy-start | bytes 6291460
  100.2 7.0 %copy-start.36 = (bf16[1,1024,256]{2,1,0:T(8,128)(2,1)S(1)}, bf16[1,1024,256]{2,1,0:T(8,128)(2,1)}, u32[]{:S(2)}) copy-start(bf16[1,1024,256]{2,1,0:T(8,128)(2,1)} %fusion.71) | copy-start | bytes 1572868
  107.2 95.9 %reduce-scatter.8.cloned.1.call-start = ((), (), s32[]{:S(2)}) async-start(), calls=%async_computation.4 | async-start | bytes 1310720 | tf_op jit(solution)/shard_map/reduce_scatter | solution.py:154
  108.3 94.8 %reduce-scatter.6.cloned.1.call-start = ((), (), s32[]{:S(2)}) async-start(), calls=%async_computation.3 | async-start | bytes 1310720 | tf_op jit(solution)/shard_map/reduce_scatter | solution.py:151
  113.7 83.8 %collective-permute-start.6 = (bf16[1,2,64,256]{3,2,1,0:T(8,128)(2,1)S(1)}, bf16[1,2,64,256]{3,2,1,0:T(8,128)(2,1)S(1)}, u32[]{:S(2)}, u32[]{:S(2)}) collective-permute-start(bf16[1,2,64,256]{3,2,1,0:T(8,128)(2,1)S(1)} %get-tuple-element.91), channel_id=1, source_target_pairs={{0,1},{1,2},{2,3},{3,4},{4,5},{5,6},{6,7},{7,8},{8,9},{9,10},{10,1... | collective-permute-start | bytes 196616 | tf_op jit(solution)/shard_map/ppermute | solution.py:17
  116.9 80.6 %collective-permute-start.7 = (bf16[1,2,64,256]{3,2,1,0:T(8,128)(2,1)S(1)}, bf16[1,2,64,256]{3,2,1,0:T(8,128)(2,1)S(1)}, u32[]{:S(2)}, u32[]{:S(2)}) collective-permute-start(bf16[1,2,64,256]{3,2,1,0:T(8,128)(2,1)S(1)} %get-tuple-element.92), channel_id=1, source_target_pairs={{1,0},{2,1},{3,2},{4,3},{5,4},{6,5},{7,6},{8,7},{9,8},{10,9},{11,1... | collective-permute-start | bytes 196616 | tf_op jit(solution)/shard_map/ppermute | solution.py:17
  124.0 180.0 %all-reduce.7.cloned.1.call-start = ((), (), s32[]{:S(2)}) async-start(), calls=%async_computation.6 | async-start | bytes 1048576 | tf_op jit(solution)/shard_map/psum | solution.py:146
  203.1 103.0 %copy-start.1 = (f32[1000,256]{1,0:T(8,128)S(1)}, f32[1000,256]{1,0:T(8,128)}, u32[]{:S(2)}) copy-start(f32[1000,256]{1,0:T(8,128)} %param.15) | copy-start | bytes 3072004
  (35 other events, 111.9 us)
Sparse Core Ops, SparseCore 0:
  107.3 23.4 reduce-scatter.9
  133.3 24.0 reduce-scatter.7
  160.4 23.1 reduce-scatter.5
  203.2 100.7 all-reduce.6
where the time goes:
time: 314 us; the launch traced here: 313 us
  waiting for transfers between devices  111 us (35%)
  blocking collectives  65.2 us (21%)
  matrix products  45.3 us (14%)
  other arithmetic  31 us (10%)
  local copies, waits for them, and re-layouts  22.7 us (7%)
  starting transfers between devices  21.2 us (7%)
  between operations  16.4 us (5%)
    psum x1, waiting for transfers between devices, on_device(): lax.psum(local_up.astype(jnp.bfloat16), 'space').astype(jnp.float32)  99.6 us
    psum x1, blocking collectives, on_device(): lax.psum(local_depth.astype(jnp.bfloat16), 'space').astype(jnp.float32)  65.2 us
    ppermute x8, starting transfers between devices, from_behind(): lax.ppermute(value, axis, [(source, source + steps) for source in range(i...  21.1 us
    unnamed x102, local copies, waits for them, and re-layouts  12.1 us
    dot_general x2, matrix products, on_device(): lax.dot_general(flat_grad, w_down[block], contract_cols, preferred_elemen...  11.8 us
    dot_general x2, matrix products, on_device(): lax.dot_general(d_preact, w_up[block], contract_cols, preferred_element_t...  10.1 us
    dot_general x2, matrix products, on_device(): lax.dot_general(hidden, flat_grad, contract_rows, preferred_element_type=...  9.67 us
    dot_general x2, matrix products, on_device(): lax.dot_general(activation, d_preact, contract_rows, preferred_element_ty...  8.18 us
  transfers between devices with their start and end apart: 12, of which 4 were waited for; matrix products, arithmetic and copies ran while one was open for 9% of the time, Pallas kernels for 0%

commit v1 on v0

--- a/solution.py
+++ b/solution.py
@@ -9,6 +9,12 @@
 ROOT = math.sqrt(2.0 / math.pi)
 FORWARD_ORDER = (0, 1, 2, 3, 4, 5, 6)
 MIRROR_ORDER = (0, 2, 1, 4, 3, 6, 5)
+
+
+def gather_and_add(x, axis):
+    parts = lax.all_gather(x, axis, axis=0, tiled=False)
+    total = parts.sum(axis=0)
+    return total
 
 
 def from_behind(value, axis, steps):
@@ -143,7 +149,7 @@
     local_down = jnp.stack(parts_down)
     local_depth = jnp.stack(parts_depth)
     whole = (
-        lax.psum(local_up.astype(jnp.bfloat16), "space").astype(jnp.float32),
+        gather_and_add(local_up.astype(jnp.bfloat16), "space").astype(jnp.float32),
         lax.psum(local_down.astype(jnp.bfloat16), "space").astype(jnp.float32),
         lax.psum(local_depth.astype(jnp.bfloat16), "space").astype(jnp.float32),
     )

time: 314 us -> 351 us (1.12)
  waiting for transfers between devices: 111 us -> 132 us
  other arithmetic: 31 us -> 46.3 us
    all_gather x0 -> x1, waiting for transfers between devices: none -> 33.8 us  [gather_and_add(): parts = lax.all_gather(x, axis, axis=0, tiled=False)]
    psum x1, waiting for transfers between devices: 99.6 us -> 86.7 us  [on_device(): lax.psum(local_down.astype(jnp.bfloat16), 'space').astype(jnp.float32)]
    reduce_sum x0 -> x1, other arithmetic: none -> 12.6 us  [gather_and_add(): total = parts.sum(axis=0)]
  transfers between devices with their start and end apart: 12 -> 13, of which waited for: 4 -> 5; matrix products, arithmetic and copies ran while one was open for 9% -> 12% of each run, Pallas kernels for 0% -> 0%
where the time goes in v1:
time: 351 us; the launch traced here: 350 us
  waiting for transfers between devices  132 us (38%)
  blocking collectives  66.4 us (19%)
  other arithmetic  46.3 us (13%)
  matrix products  42 us (12%)
  local copies, waits for them, and re-layouts  24.7 us (7%)
  starting transfers between devices  21.3 us (6%)
  between operations  17.8 us (5%)
    psum x1, waiting for transfers between devices, on_device(): lax.psum(local_down.astype(jnp.bfloat16), 'space').astype(jnp.float32)  86.7 us
    psum x1, blocking collectives, on_device(): lax.psum(local_depth.astype(jnp.bfloat16), 'space').astype(jnp.float32)  66.4 us
    all_gather x1, waiting for transfers between devices, gather_and_add(): parts = lax.all_gather(x, axis, axis=0, tiled=False)  33.8 us
    ppermute x8, starting transfers between devices, from_behind(): lax.ppermute(value, axis, [(source, source + steps) for source in range(i...  21.1 us
    reduce_sum x1, other arithmetic, gather_and_add(): total = parts.sum(axis=0)  12.6 us
    unnamed x102, local copies, waits for them, and re-layouts  12.1 us
    dot_general x2, matrix products, on_device(): lax.dot_general(flat_grad, w_down[block], contract_cols, preferred_elemen...  11.8 us
    dot_general x2, matrix products, on_device(): lax.dot_general(d_preact, w_up[block], contract_cols, preferred_element_t...  10.1 us
  transfers between devices with their start and end apart: 13, of which 5 were waited for; matrix products, arithmetic and copies ran while one was open for 12% of the time, Pallas kernels for 0%

profile of v1, /device:TPU:1, one launch (start us, length us, event | category | flops | bytes accessed | tf_op | source)
XLA Modules:
  0.0 350.2 jit_solution(6651649523426975879)
XLA Ops:
  8.8 3.4 multiply_convert_fusion.6
  13.1 4.6 %collective-permute-start = (bf16[1,2,64,256]{3,2,1,0:T(8,128)(2,1)S(1)}, bf16[1,2,64,256]{3,2,1,0:T(8,128)(2,1)S(1)}, u32[]{:S(2)}, u32[]{:S(2)}) collective-permute-start(bf16[1,2,64,256]{3,2,1,0:T(8,128)(2,1)S(1)} %get-tuple-element.95), channel_id=1, source_target_pairs={{0,1},{1,2},{2,3},{3,4},{4,5},{5,6},{6,7},{7,8},{8,9},{9,10},{10,1... | collective-permute-start | bytes 196616 | tf_op jit(solution)/shard_map/ppermute | solution.py:23
  17.7 1.9 collective-permute-start.1
  33.1 3.0 convolution_add_fusion
  38.5 2.4 collective-permute-start.2
  41.0 2.1 collective-permute-start.3
  43.4 3.2 collective-permute-done.3
  54.4 2.2 fusion.22
  58.5 5.9 %fusion.8 = bf16[2048,1024]{1,0:T(8,128)(2,1)S(1)} fusion(f32[2048,1024]{1,0:T(8,128)S(1)} %fusion.76, bf16[2048,256]{1,0:T(8,128)(2,1)S(1)} %bitcast.382, bf16[2,1024,256]{2,1,0:T(8,128)(2,1)S(1)} %copy-done.39), kind=kOutput, calls=%fused_computation.20 | convolution fusion | flops 1113587712 | bytes 14155776 | tf_op jit(solution)/shard_map/dot_general | solution.py:130
  64.5 4.3 %fusion.38 = (bf16[256]{0:T(256)(128)(2,1)S(1)}, bf16[256]{0:T(256)(128)(2,1)S(1)}, bf16[256]{0:T(256)(128)(2,1)S(1)}, bf16[256]{0:T(256)(128)(2,1)S(1)}, bf16[2...) fusion(f32[4,8,8,8,256]{4,3,2,1,0:T(8,128)S(1)} %copy.124, ...), kind=kOutput, calls=%fused_computation.80 | convolution fusion | flops 1083701504 | bytes 20459008 | tf_op jit(solution)/shard_map/dot_general | solution.py:137
  70.4 1.9 collective-permute-start.4
  72.3 2.8 collective-permute-start.5
  75.1 6.1 %fusion.71 = bf16[1,1024,256]{2,1,0:T(8,128)(2,1)} fusion(bf16[2048,256]{1,0:T(8,128)(2,1)S(1)} %bitcast.383, f32[2048,1024]{1,0:T(8,128)} %copy-done.3), kind=kOutput, calls=%fused_computation.168 | convolution fusion | flops 1092878336 | bytes 9961472 | tf_op jit(solution)/shard_map/dot_general | solution.py:127
  88.9 2.2 fusion.31
  91.2 3.6 %fusion.74 = bf16[1,1024,256]{2,1,0:T(8,128)(2,1)S(1)} fusion(bf16[2048,256]{1,0:T(8,128)(2,1)S(1)} %fusion.31, f32[2048,1024]{1,0:T(8,128)S(1)} %bitcast.361), kind=kOutput, calls=%fused_computation.171 | convolution fusion | flops 1092878336 | bytes 9961472 | tf_op jit(solution)/shard_map/dot_general | solution.py:127
  94.9 5.9 %fusion.13 = bf16[2048,1024]{1,0:T(8,128)(2,1)S(1)} fusion(f32[2048,1024]{1,0:T(8,128)S(1)} %bitcast.361, bf16[2048,256]{1,0:T(8,128)(2,1)S(1)} %fusion.31, bf16[2,1024,256]{2,1,0:T(8,128)(2,1)S(1)} %copy-done.40), kind=kOutput, calls=%fused_computation.25 | convolution fusion | flops 1113587712 | bytes 14155776 | tf_op jit(solution)/shard_map/dot_general | solution.py:130
  101.0 5.9 %fusion.52 = (bf16[256]{0:T(256)(128)(2,1)S(1)}, bf16[256]{0:T(256)(128)(2,1)S(1)}, bf16[256]{0:T(256)(128)(2,1)S(1)}, bf16[256]{0:T(256)(128)(2,1)S(1)}, bf16[2...) fusion(f32[4,8,8,8,256]{4,3,2,1,0:T(8,128)S(1)} %copy-done.12, ...), kind=kOutput, calls=%fused_computation.94 | convolution fusion | flops 1090517248 | bytes 20459008 | tf_op jit(solution)/shard_map/dot_general | solution.py:137
  109.2 3.6 %fusion.73 = bf16[1,1,256,1024]{3,2,1,0:T(8,128)(2,1)S(1)} fusion(bf16[2048,256]{1,0:T(8,128)(2,1)S(1)} %copy-done.26, bf16[2048,1024]{1,0:T(8,128)(2,1)} %copy-done.31), kind=kOutput, calls=%fused_computation.170 | convolution fusion | flops 1074003968 | bytes 5767168 | tf_op jit(solution)/shard_map/dot_general | solution.py:134
  119.5 3.4 collective-permute-start.6
  124.8 6.7 %reduce-scatter.10.cloned.1.call-done = bf16[64,14]{1,0:T(8,128)(2,1)} async-done(((bf16[256,14]{1,0:T(8,128)(2,1)}), bf16[64,14]{1,0:T(8,128)(2,1)}) %reduce-scatter.10.cloned.1.call-update) | async-done | bytes 1808
  132.5 66.4 %psum.17 = bf16[2,7,64]{2,1,0:T(8,128)(2,1)S(1)} all-reduce(bf16[2,7,64]{2,1,0:T(8,128)(2,1)S(1)} %copy.135), channel_id=1, replica_groups=mesh['rep'=4,'space'=32] {'space'}, use_global_device_ids=true, to_apply=%region_18.19 | all-reduce | flops 896 | bytes 3584 | tf_op jit(solution)/shard_map/psum | solution.py:154
  202.4 33.8 %all-gather.2.cloned.1.call-done = bf16[32,2,256,1024]{3,2,1,0:T(8,128)(2,1)} async-done(((bf16[1,2,256,1024]{3,2,1,0:T(8,128)(2,1)}), bf16[32,2,256,1024]{3,2,1,0:T(8,128)(2,1)}) %all-gather.2.cloned.1.call-update) | async-done | bytes 33554448 | tf_op jit(solution)/shard_map/all_gather | solution.py:15
  236.1 12.6 %reduce_sum.138 = bf16[2,256,1024]{2,1,0:T(8,128)(2,1)} reduce(bf16[32,2,256,1024]{3,2,1,0:T(8,128)(2,1)} %all-gather.2.cloned.1.call-done, bf16[]{:T(256)} %constant.12.clone.1), dimensions={0}, to_apply=%region_0.1 | reduce | flops 16252928 | bytes 34603008 | tf_op jit(solution)/shard_map/reduce_sum | solution.py:16
  252.8 86.7 %all-reduce.6.cloned.1.call-done = bf16[2,256,256]{2,1,0:T(8,128)(2,1)} async-done(((bf16[2,256,256]{2,1,0:T(8,128)(2,1)}), bf16[2,256,256]{2,1,0:T(8,128)(2,1)}) %all-reduce.6.cloned.1.call-update) | async-done | bytes 262160 | tf_op jit(solution)/shard_map/psum | solution.py:153
  (217 shorter events, 57.8 us)
Async XLA Ops:
  8.0 14.0 %copy-start = (f32[1000,256]{1,0:T(8,128)S(1)}, f32[1000,256]{1,0:T(8,128)}, u32[]{:S(2)}) copy-start(f32[1000,256]{1,0:T(8,128)} %param.15) | copy-start | bytes 3072004
  8.0 123.5 %reduce-scatter.10.cloned.1.call-start = ((), (), s32[]{:S(2)}) async-start(), calls=%async_computation.7 | async-start | bytes 81920
  12.2 14.9 %copy-start.4 = (bf16[4,512,256]{2,1,0:T(8,128)(2,1)}, bf16[4,512,256]{2,1,0:T(8,128)(2,1)S(1)}, u32[]{:S(2)}) copy-start(bf16[4,512,256]{2,1,0:T(8,128)(2,1)S(1)} %get-tuple-element.112) | copy-start | bytes 3145732
  12.5 9.4 %copy-start.37 = (s32[4,4]{1,0:T(4,128)S(1)}, s32[4,4]{1,0:T(4,128)}, u32[]{:S(2)}) copy-start(s32[4,4]{1,0:T(4,128)} %param.19) | copy-start | bytes 196
  12.5 9.5 %copy-start.36 = (f32[2,7,256]{2,0,1:T(2,128)S(1)}, f32[2,7,256]{2,0,1:T(2,128)}, u32[]{:S(2)}) copy-start(f32[2,7,256]{2,0,1:T(2,128)} %param.14) | copy-start | bytes 43012
  13.1 9.0 %collective-permute-start = (bf16[1,2,64,256]{3,2,1,0:T(8,128)(2,1)S(1)}, bf16[1,2,64,256]{3,2,1,0:T(8,128)(2,1)S(1)}, u32[]{:S(2)}, u32[]{:S(2)}) collective-permute-start(bf16[1,2,64,256]{3,2,1,0:T(8,128)(2,1)S(1)} %get-tuple-element.95), channel_id=1, source_target_pairs={{0,1},{1,2},{2,3},{3,4},{4,5},{5,6},{6,7},{7,8},{8,9},{9,10},{10,1... | collective-permute-start | bytes 196616 | tf_op jit(solution)/shard_map/ppermute | solution.py:23
  17.7 5.6 %collective-permute-start.1 = (bf16[1,2,64,256]{3,2,1,0:T(8,128)(2,1)S(1)}, bf16[1,2,64,256]{3,2,1,0:T(8,128)(2,1)S(1)}, u32[]{:S(2)}, u32[]{:S(2)}) collective-permute-start(bf16[1,2,64,256]{3,2,1,0:T(8,128)(2,1)S(1)} %get-tuple-element.96), channel_id=1, source_target_pairs={{1,0},{2,1},{3,2},{4,3},{5,4},{6,5},{7,6},{8,7},{9,8},{10,9},{11,1... | collective-permute-start | bytes 196616 | tf_op jit(solution)/shard_map/ppermute | solution.py:23
  38.5 4.8 %collective-permute-start.2 = (bf16[1,2,64,256]{3,2,1,0:T(8,128)(2,1)S(1)}, bf16[1,2,64,256]{3,2,1,0:T(8,128)(2,1)S(1)}, u32[]{:S(2)}, u32[]{:S(2)}) collective-permute-start(bf16[1,2,64,256]{3,2,1,0:T(8,128)(2,1)S(1)} %get-tuple-element.93), channel_id=1, source_target_pairs={{0,1},{1,2},{2,3},{3,4},{4,5},{5,6},{6,7},{7,8},{8,9},{9,10},{10,1... | collective-permute-start | bytes 196616 | tf_op jit(solution)/shard_map/ppermute | solution.py:23
  41.0 5.6 %collective-permute-start.3 = (bf16[1,2,64,256]{3,2,1,0:T(8,128)(2,1)S(1)}, bf16[1,2,64,256]{3,2,1,0:T(8,128)(2,1)S(1)}, u32[]{:S(2)}, u32[]{:S(2)}) collective-permute-start(bf16[1,2,64,256]{3,2,1,0:T(8,128)(2,1)S(1)} %get-tuple-element.94), channel_id=1, source_target_pairs={{1,0},{2,1},{3,2},{4,3},{5,4},{6,5},{7,6},{8,7},{9,8},{10,9},{11,1... | collective-permute-start | bytes 196616 | tf_op jit(solution)/shard_map/ppermute | solution.py:23
  57.9 6.5 %copy-start.3 = (f32[2048,1024]{1,0:T(8,128)}, f32[2048,1024]{1,0:T(8,128)S(1)}, u32[]{:S(2)}) copy-start(f32[2048,1024]{1,0:T(8,128)S(1)} %fusion.76) | copy-start | bytes 25165828
  68.8 6.4 %copy-start.28 = (bf16[4,512,256]{2,1,0:T(8,128)(2,1)S(1)}, bf16[4,512,256]{2,1,0:T(8,128)(2,1)}, u32[]{:S(2)}) copy-start(bf16[4,512,256]{2,1,0:T(8,128)(2,1)} %get-tuple-element.111) | copy-start | bytes 3145732
  70.4 12.5 %collective-permute-start.4 = (bf16[1,2,64,256]{3,2,1,0:T(8,128)(2,1)S(1)}, bf16[1,2,64,256]{3,2,1,0:T(8,128)(2,1)S(1)}, u32[]{:S(2)}, u32[]{:S(2)}) collective-permute-start(bf16[1,2,64,256]{3,2,1,0:T(8,128)(2,1)S(1)} %get-tuple-element.91), channel_id=1, source_target_pairs={{0,1},{1,2},{2,3},{3,4},{4,5},{5,6},{6,7},{7,8},{8,9},{9,10},{10,1... | collective-permute-start | bytes 196616 | tf_op jit(solution)/shard_map/ppermute | solution.py:23
  72.3 8.9 %copy-start.8 = (bf16[2048,256]{1,0:T(8,128)(2,1)S(1)}, bf16[2048,256]{1,0:T(8,128)(2,1)}, u32[]{:S(2)}) copy-start(bf16[2048,256]{1,0:T(8,128)(2,1)} %copy-done.7) | copy-start | bytes 3145732
  72.3 10.6 %collective-permute-start.5 = (bf16[1,2,64,256]{3,2,1,0:T(8,128)(2,1)S(1)}, bf16[1,2,64,256]{3,2,1,0:T(8,128)(2,1)S(1)}, u32[]{:S(2)}, u32[]{:S(2)}) collective-permute-start(bf16[1,2,64,256]{3,2,1,0:T(8,128)(2,1)S(1)} %get-tuple-element.92), channel_id=1, source_target_pairs={{1,0},{2,1},{3,2},{4,3},{5,4},{6,5},{7,6},{8,7},{9,8},{10,9},{11,1... | collective-permute-start | bytes 196616 | tf_op jit(solution)/shard_map/ppermute | solution.py:23
  94.8 6.0 %copy-start.6 = (bf16[4,512,256]{2,1,0:T(8,128)(2,1)S(1)}, bf16[4,512,256]{2,1,0:T(8,128)(2,1)}, u32[]{:S(2)}) copy-start(bf16[4,512,256]{2,1,0:T(8,128)(2,1)} %copy-done.4) | copy-start | bytes 3145732
  94.9 6.0 %copy-start.10 = (f32[4,8,8,8,256]{4,3,2,1,0:T(8,128)S(1)}, f32[4,8,8,8,256]{4,3,2,1,0:T(8,128)}, u32[]{:S(2)}) copy-start(f32[4,8,8,8,256]{4,3,2,1,0:T(8,128)} %copy-done.9) | copy-start | bytes 6291460
  100.9 7.0 %copy-start.35 = (bf16[1,1024,256]{2,1,0:T(8,128)(2,1)S(1)}, bf16[1,1024,256]{2,1,0:T(8,128)(2,1)}, u32[]{:S(2)}) copy-start(bf16[1,1024,256]{2,1,0:T(8,128)(2,1)} %fusion.71) | copy-start | bytes 1572868
  107.9 91.6 %reduce-scatter.8.cloned.1.call-start = ((), (), s32[]{:S(2)}) async-start(), calls=%async_computation.5 | async-start | bytes 1310720 | tf_op jit(solution)/shard_map/reduce_scatter | solution.py:160
  109.1 127.0 %all-gather.2.cloned.1.call-start = ((), (), s32[]{:S(2)}) async-start(), calls=%async_computation.3 | async-start | bytes 34603008 | tf_op jit(solution)/shard_map/all_gather | solution.py:15
  115.3 224.2 %all-reduce.6.cloned.1.call-start = ((), (), s32[]{:S(2)}) async-start(), calls=%async_computation.6 | async-start | bytes 524288 | tf_op jit(solution)/shard_map/psum | solution.py:153
  119.5 80.1 %collective-permute-start.6 = (bf16[1,2,64,256]{3,2,1,0:T(8,128)(2,1)S(1)}, bf16[1,2,64,256]{3,2,1,0:T(8,128)(2,1)S(1)}, u32[]{:S(2)}, u32[]{:S(2)}) collective-permute-start(bf16[1,2,64,256]{3,2,1,0:T(8,128)(2,1)S(1)} %get-tuple-element.89), channel_id=1, source_target_pairs={{0,1},{1,2},{2,3},{3,4},{4,5},{5,6},{6,7},{7,8},{8,9},{9,10},{10,1... | collective-permute-start | bytes 196616 | tf_op jit(solution)/shard_map/ppermute | solution.py:23
  122.9 76.7 %collective-permute-start.7 = (bf16[1,2,64,256]{3,2,1,0:T(8,128)(2,1)S(1)}, bf16[1,2,64,256]{3,2,1,0:T(8,128)(2,1)S(1)}, u32[]{:S(2)}, u32[]{:S(2)}) collective-permute-start(bf16[1,2,64,256]{3,2,1,0:T(8,128)(2,1)S(1)} %get-tuple-element.90), channel_id=1, source_target_pairs={{1,0},{2,1},{3,2},{4,3},{5,4},{6,5},{7,6},{8,7},{9,8},{10,9},{11,1... | collective-permute-start | bytes 196616 | tf_op jit(solution)/shard_map/ppermute | solution.py:23
  199.5 141.8 %reduce-scatter.6.cloned.1.call-start = ((), (), s32[]{:S(2)}) async-start(), calls=%async_computation.4 | async-start | bytes 1310720 | tf_op jit(solution)/shard_map/reduce_scatter | solution.py:157
  251.6 91.5 %copy-start.1 = (f32[1000,256]{1,0:T(8,128)S(1)}, f32[1000,256]{1,0:T(8,128)}, u32[]{:S(2)}) copy-start(f32[1000,256]{1,0:T(8,128)} %param.15) | copy-start | bytes 3072004
  (36 other events, 116.9 us)
Sparse Core Ops, SparseCore 0:
  108.0 23.4 reduce-scatter.9
  134.1 24.1 reduce-scatter.7
  248.8 20.5 reduce-scatter.5
Sparse Core Ops, SparseCore 1:
  115.4 120.7 all-gather.1
  239.6 99.9 all-reduce.5
